TPU v7x, 32 devices: a whole 2x2x4 slice. The times are simulated.
32 devices in a mesh: pipe: 4 (over y, x), tensor: 4 (over z), dp: 2 (over core).
Axes of the slice: x: 2, y: 2, z: 4, core: 2. Of those that a mesh axis runs over, the one named last changes fastest.
Arguments:
- hidden: bfloat16 [512, 5120], P('dp', ('pipe', 'tensor')), may hold values from -16 to 16
- head_weight: bfloat16 [18992, 5120], P(('pipe', 'tensor'), 'dp'), may hold values from -2 to 2
- labels: int32 [512], P('dp'), may hold values from 0 to 18991
- loss_weight: float32 [512], P('dp'), may hold values from 1 to 10
Outputs:
- hidden_grad: bfloat16 [512, 5120], P('dp', ('pipe', 'tensor'))
- head_grad: bfloat16 [18992, 5120], P(('pipe', 'tensor'), 'dp')
- token_loss: float32 [512], P('dp')
All inputs are finite; a program needn't handle non-finite values.
Results may differ from a plain program's by a relative error of at most 0.0052.
Values may be sent and summed in bfloat16 or wider, within the bound.
A program may use at most 128 MiB of HBM per device.

v0:
```python
import functools

import jax
import jax.numpy as jnp
from jax import lax
from jax.experimental import pallas as pl
from jax.experimental.pallas import tpu as pltpu
from jax.sharding import PartitionSpec as P

GROUP = ("pipe", "tensor")
MESH = pl.DeviceIdType.MESH
VMEM = pl.BlockSpec(memory_space=pltpu.VMEM)
ANY = pl.BlockSpec(memory_space=pl.ANY)
VMEM_BYTES = 48 * 1024 * 1024
Z = 4


def spans(rows, size):
    return [(start, min(size, rows - start)) for start in range(0, rows, size)]


class Place:
    def __init__(self):
        pipe = lax.axis_index("pipe")
        self.pipe = pipe
        self.x, self.y = pipe % 2, pipe // 2
        self.z = lax.axis_index("tensor")
        self.core = lax.axis_index("dp")
        self.home = self.y == self.core
        self.away = self.y == 1 - self.core
        self.x_peer = {"pipe": self.y * 2 + 1 - self.x}
        self.y_peer = {"pipe": (1 - self.y) * 2 + self.x}
        self.up = {"tensor": self.z + 1}
        self.down = {"tensor": self.z - 1}
        self.mate = {"dp": 1 - self.core}


def remote(src, dst, send_sem, recv_sem, device):
    return pltpu.make_async_remote_copy(
        src_ref=src, dst_ref=dst, send_sem=send_sem, recv_sem=recv_sem, device_id=device, device_id_type=MESH
    )


def greet_group(me, n):
    barrier = pltpu.get_barrier_semaphore()
    index = me.pipe * Z + me.z

    def greet(step, carry):
        other = (index + step) % n
        pl.semaphore_signal(
            barrier, inc=1, device_id={"pipe": other // Z, "tensor": other % Z}, device_id_type=MESH
        )
        return carry

    lax.fori_loop(1, n, greet, 0)
    pl.semaphore_signal(barrier, inc=1, device_id=me.mate, device_id_type=MESH)
    pl.semaphore_wait(barrier, n)


def forward_kernel(
    n, block, piece, weight, labels_in, loss_weight_in,
    features_out, grad_out, loss_out,
    features, weight_here, partial, partial_in, grad_here, stats, labels, loss_weight,
    recv, recv_low, send_up, send_down, low_up, low_down, send_x, send_y, send_y2, own_sem, weight_sem,
    mate_sems, stat_send, stat_recv, out_sems, token_sems,
):
    me = Place()
    tokens = piece.shape[1]
    rows = weight.shape[0]
    x, z, core = me.x, me.z, me.core
    load_weight = pltpu.make_async_copy(weight, weight_here, weight_sem)
    load_weight.start()
    load_tokens = [
        pltpu.make_async_copy(labels_in, labels, token_sems.at[0]),
        pltpu.make_async_copy(loss_weight_in, loss_weight, token_sems.at[1]),
    ]
    for load in load_tokens:
        load.start()
    greet_group(me, n)
    low = block // 80 * 16
    whole, upper, lower = (0, block), (low, block - low), (0, low)

    def at(column, level, half, part):
        start = pl.multiple_of((column * Z + level) * block + part[0], 16)
        return features.at[pl.ds(start, part[1]), pl.ds(pl.multiple_of(half * tokens, tokens), tokens)]

    def copy(column, level, half, send_sem, device, part):
        here = at(column, level, half, part)
        sems = recv_low if part is lower else recv
        return remote(here, here, send_sem, sems.at[(column * Z + level) * 2 + half], device)

    def arrived(column, level, half, part):
        copy(column, level, half, send_y.at[0], me.mate, part).wait_recv()

    def run(transfer):
        if waiting:
            transfer.wait_send()
        else:
            transfer.start()

    def need(column, level, half, part):
        if not waiting:
            arrived(column, level, half, part)

    def line_sends(level, half, sign, part):
        slot = level * 2 + half
        if sign <= 0:
            pl.when(z < Z - 1)(lambda: run(copy(x, level, half, send_up.at[slot], me.up, upper)))
        if sign >= 0:
            pl.when(z > 0)(lambda: run(copy(x, level, half, send_down.at[slot], me.down, upper)))
        run(copy(x, level, half, send_x.at[slot], me.x_peer, part))
        run(copy(x, level, half, send_y.at[slot], me.y_peer, part))

    def line_step(distance, sign):
        level = z + sign * distance

        def home():
            for half in (0, 1):
                need(x, level, half, upper)
                line_sends(level, half, sign, upper)

        def away():
            need(x, level, 0, upper)
            run(copy(x, level, 0, send_x.at[level * 2], me.x_peer, upper))
            need(x, level, 1, upper)

        valid = (level >= 0) & (level < Z)
        pl.when(valid & me.home)(home)
        pl.when(valid & me.away)(away)

    def first_step():
        @pl.when(me.home)
        def _():
            line_sends(z, core, 0, whole)
            need(x, z, 1 - core, whole)
            line_sends(z, 1 - core, 0, whole)

        @pl.when(me.away)
        def _():
            need(x, z, 0, whole)
            run(copy(x, z, 0, send_x.at[z * 2], me.x_peer, whole))
            need(x, z, 1, whole)

    def peer_step(distance, sign):
        level = z + sign * distance
        part = upper if distance else whole
        valid = (level >= 0) & (level < Z)
        if not waiting:
            @pl.when(valid)
            def _():
                arrived(1 - x, level, 0, part)
                arrived(1 - x, level, 1, part)

        pl.when(valid & me.home)(
            lambda: run(copy(1 - x, level, 1, send_y2.at[level], me.y_peer, part))
        )

    def low_step(distance, sign):
        level = z + sign * distance

        def each(which, carry):
            column, half = which // 2, which % 2
            slot = (column * Z + level) * 2 + half
            if distance:
                need(column, level, half, lower)
            if sign <= 0:
                pl.when(z < Z - 1)(lambda: run(copy(column, level, half, low_up.at[slot], me.up, lower)))
            if sign >= 0:
                pl.when(z > 0)(lambda: run(copy(column, level, half, low_down.at[slot], me.down, lower)))
            return carry

        @pl.when((level >= 0) & (level < Z))
        def _():
            lax.fori_loop(0, 4, each, 0)

    def multiply(pair, half, first):
        width = 2 * block
        depth = pl.ds(pl.multiple_of(pair * width, width), width)
        right = features[depth, pl.ds(pl.multiple_of(half * tokens, tokens), tokens)]
        for start, size in spans(rows, 592):
            part = jnp.dot(weight_here[pl.ds(start, size), depth], right, preferred_element_type=jnp.float32)
            where = (half, pl.ds(start, size))
            partial[where] = part if first else partial[where] + part

    def multiply_both(pair, first=False):
        def step(half, carry):
            multiply(pair, half, first)
            return carry

        lax.fori_loop(0, 2, step, 0)

    waiting = False
    mine = at(x, z, core, whole)
    own_copy = pltpu.make_async_copy(piece, mine, own_sem)
    own_send = remote(piece, mine, own_sem, recv.at[(x * Z + z) * 2 + core], me.mate)
    pl.when(me.home)(own_copy.start)
    pl.when(me.away)(own_send.start)
    pl.when(me.home)(own_copy.wait)
    first_step()
    for sign in (-1, 1):
        line_step(1, sign)
    peer_step(0, 1)
    low_step(0, 0)
    for sign in (-1, 1):
        line_step(2, sign)
    for sign in (-1, 1):
        peer_step(1, sign)
    for sign in (-1, 1):
        low_step(1, sign)
    load_weight.wait()
    multiply_both(x * 2 + z // 2, True)
    for sign in (-1, 1):
        line_step(3, sign)
    for sign in (-1, 1):
        peer_step(2, sign)
    for sign in (-1, 1):
        low_step(2, sign)
    multiply_both((1 - x) * 2 + z // 2)
    for sign in (-1, 1):
        peer_step(3, sign)
    for sign in (-1, 1):
        low_step(3, sign)
    store_features = pltpu.make_async_copy(features, features_out, out_sems.at[0])
    store_features.start()
    near, far = x * 2 + 1 - z // 2, (1 - x) * 2 + 1 - z // 2
    multiply(near, 1 - core, False)
    multiply(far, 1 - core, False)
    swap = remote(partial.at[1 - core], partial_in, mate_sems.at[0], mate_sems.at[1], me.mate)
    swap.start()
    multiply(near, core, False)
    multiply(far, core, False)

    waiting = True
    pl.when(me.away)(own_send.wait_send)
    first_step()
    peer_step(0, 1)
    low_step(0, 0)
    for distance in (1, 2, 3):
        for sign in (-1, 1):
            line_step(distance, sign)
            peer_step(distance, sign)
            low_step(distance, sign)
    for load in load_tokens:
        load.wait()
    swap.wait()

    index = me.pipe * Z + z
    target = labels[...] - index * rows
    peak = jnp.full((1, tokens), -jnp.inf, jnp.float32)
    picked = jnp.zeros((1, tokens), jnp.float32)
    parts = spans(rows, 128)

    def is_target(start, size):
        return lax.broadcasted_iota(jnp.int32, (size, tokens), 0) + start == target

    for start, size in parts:
        where = pl.ds(start, size)
        logits = partial[core, where] + partial_in[where]
        partial_in[where] = logits
        peak = jnp.maximum(peak, jnp.max(logits, axis=0, keepdims=True))
        picked += jnp.sum(jnp.where(is_target(start, size), logits, 0.0), axis=0, keepdims=True)
    total = jnp.zeros((1, tokens), jnp.float32)
    for start, size in parts:
        total += jnp.sum(jnp.exp(partial_in[pl.ds(start, size)] - peak), axis=0, keepdims=True)
    stats[index] = jnp.concatenate([peak, total, picked, jnp.zeros((5, tokens), jnp.float32)], axis=0)

    def stat_copy(step):
        other = (index + step) % n
        device = {"pipe": other // Z, "tensor": other % Z}
        return remote(stats.at[index], stats.at[index], stat_send.at[step], stat_recv.at[index], device)

    def send_stat(step, carry):
        stat_copy(step).start()
        return carry

    def wait_stat(step, carry):
        other = (index + step) % n
        remote(
            stats.at[other], stats.at[other], stat_send.at[step], stat_recv.at[other], me.mate
        ).wait_recv()
        return carry

    def wait_stat_send(step, carry):
        stat_copy(step).wait_send()
        return carry

    lax.fori_loop(1, n, send_stat, 0)
    lax.fori_loop(1, n, wait_stat, 0)
    every = stats[...]
    peaks, totals, picks = every[:, 0], every[:, 1], every[:, 2]
    row_peak = jnp.max(peaks, axis=0, keepdims=True)
    row_total = jnp.sum(totals * jnp.exp(peaks - row_peak), axis=0, keepdims=True)
    loss_out[...] = row_peak + jnp.log(row_total) - jnp.sum(picks, axis=0, keepdims=True)
    scale = loss_weight[...]
    inverse = 1.0 / row_total
    for start, size in parts:
        where = pl.ds(start, size)
        share = jnp.exp(partial_in[where] - row_peak) * inverse
        hit = jnp.where(is_target(start, size), 1.0, 0.0)
        grad_here[where] = (scale * (share - hit)).astype(jnp.bfloat16)
    mine = grad_out.at[:, pl.ds(pl.multiple_of(core * tokens, tokens), tokens)]
    keep = pltpu.make_async_copy(grad_here, mine, out_sems.at[1])
    share_grad = remote(grad_here, mine, mate_sems.at[2], mate_sems.at[3], me.mate)
    share_grad.start()
    keep.start()
    lax.fori_loop(1, n, wait_stat_send, 0)
    keep.wait()
    share_grad.wait()
    store_features.wait()


def forward(hidden_t, head_weight, labels, loss_weight, n):
    block, tokens = hidden_t.shape
    rows, width = head_weight.shape
    dma = pltpu.SemaphoreType.DMA
    return pl.pallas_call(
        functools.partial(forward_kernel, n, block),
        out_shape=(
            jax.ShapeDtypeStruct((width, 2 * tokens), jnp.bfloat16),
            jax.ShapeDtypeStruct((rows, 2 * tokens), jnp.bfloat16),
            jax.ShapeDtypeStruct((1, tokens), jnp.float32),
        ),
        in_specs=[ANY, ANY, ANY, ANY],
        out_specs=(ANY, ANY, VMEM),
        scratch_shapes=[
            pltpu.VMEM((width, 2 * tokens), jnp.bfloat16),
            pltpu.VMEM((rows, width), jnp.bfloat16),
            pltpu.VMEM((2, rows, tokens), jnp.float32),
            pltpu.VMEM((rows, tokens), jnp.float32),
            pltpu.VMEM((rows, tokens), jnp.bfloat16),
            pltpu.VMEM((n, 8, tokens), jnp.float32),
            pltpu.VMEM((1, tokens), jnp.int32),
            pltpu.VMEM((1, tokens), jnp.float32),
            dma((16,)), dma((16,)), dma((8,)), dma((8,)), dma((16,)), dma((16,)), dma((8,)), dma((8,)), dma((4,)),
            dma, dma, dma((4,)), dma((n,)), dma((n,)), dma((2,)), dma((2,)),
        ],
        compiler_params=pltpu.CompilerParams(
            collective_id=0, has_side_effects=True, vmem_limit_bytes=VMEM_BYTES
        ),
    )(hidden_t, head_weight, labels, loss_weight)


def reduce_kernel(
    block, term, out,
    from_y, from_x, from_below, from_above, passed, summed, final, landed,
    recv_y, recv_x, recv_below, recv_above, recv_final,
    send_x, send_pass, send_y, send_z, send_final,
):
    me = Place()
    tokens = out.shape[1]
    x, z, core = me.x, me.z, me.core
    barrier = pltpu.get_barrier_semaphore()
    for peer in (me.x_peer, me.y_peer, me.mate):
        pl.semaphore_signal(barrier, inc=1, device_id=peer, device_id_type=MESH)

    @pl.when(z > 0)
    def _():
        pl.semaphore_signal(barrier, inc=1, device_id=me.down, device_id_type=MESH)

    @pl.when(z < Z - 1)
    def _():
        pl.semaphore_signal(barrier, inc=1, device_id=me.up, device_id_type=MESH)

    pl.semaphore_wait(barrier, 3 + (z + Z - 1) // Z + (2 * (Z - 1) - z) // Z)

    def own(column, level, half):
        start = pl.multiple_of((column * Z + level) * block, block)
        return term.at[pl.ds(start, block), pl.ds(pl.multiple_of(half * tokens, tokens), tokens)]

    upper = z // 2
    order = (3 * (1 - upper), 2 - upper, 1 - z + 4 * upper, z)

    def away_cross(level):
        return remote(own(1 - x, level, 0), from_x.at[level * 2], send_x.at[level], recv_x.at[level * 2], me.x_peer)

    def away_diagonal(level):
        return remote(own(1 - x, level, 1), from_y.at[8 + level], send_y.at[8 + level], recv_y.at[8 + level], me.y_peer)

    def away_line(level, half):
        slot = level * 2 + half
        source = own(x, level, 1) if half else passed.at[level]
        return remote(source, from_y.at[slot], send_y.at[slot], recv_y.at[slot], me.y_peer)

    def home_cross(level, half):
        slot = level * 2 + half
        source = passed.at[level] if half else own(1 - x, level, 0)
        sem = send_pass.at[level] if half else send_x.at[level]
        return remote(source, from_x.at[slot], sem, recv_x.at[slot], me.x_peer)

    def rise(level, half):
        slot = level * 2 + half
        return remote(summed.at[slot], from_below.at[slot], send_z.at[slot], recv_below.at[slot], me.up)

    def sink(level, half):
        slot = level * 2 + half
        return remote(summed.at[slot], from_above.at[slot], send_z.at[slot], recv_above.at[slot], me.down)

    def hand_over():
        return remote(final, landed, send_final, recv_final, me.mate)

    def f32(ref):
        return ref[...].astype(jnp.float32)

    @pl.when(me.away)
    def _():
        away_cross(order[0]).start()
        away_diagonal(order[0]).start()
        for at, level in enumerate(order):
            away_line(level, 1).start()
            if at + 1 < Z:
                away_cross(order[at + 1]).start()
                away_diagonal(order[at + 1]).start()
            away_cross(level).wait_recv()
            passed[level] = (f32(own(x, level, 0)) + f32(from_x.at[level * 2])).astype(jnp.bfloat16)
            away_line(level, 0).start()
        for level in order:
            away_cross(level).wait_send()
            away_diagonal(level).wait_send()
            away_line(level, 1).wait_send()
            away_line(level, 0).wait_send()
        hand_over().wait_recv()
        out[...] = landed[...]

    @pl.when(me.home)
    def _():
        def pass_on(level):
            away_diagonal(level).wait_recv()
            passed[level] = (f32(own(1 - x, level, 1)) + f32(from_y.at[8 + level])).astype(jnp.bfloat16)
            home_cross(level, 1).start()

        def gather(level, half):
            slot = level * 2 + half
            for inbox, sems in ((from_y, recv_y), (from_x, recv_x)):
                remote(final, inbox.at[slot], send_final, sems.at[slot], me.mate).wait_recv()
            return f32(own(x, level, half)) + f32(from_y.at[slot]) + f32(from_x.at[slot])

        def send_on(level):
            for half in (1, 0):
                slot = level * 2 + half
                total = gather(level, half)
                summed[slot] = total.astype(jnp.bfloat16)

                @pl.when((level < z) & (z < Z - 1))
                def _():
                    sink(level, half).wait_recv()
                    summed[slot] = (total + f32(from_above.at[slot])).astype(jnp.bfloat16)

                @pl.when((level > z) & (z > 0))
                def _():
                    rise(level, half).wait_recv()
                    summed[slot] = (total + f32(from_below.at[slot])).astype(jnp.bfloat16)

                pl.when(level < z)(lambda: sink(level, half).start())
                pl.when(level > z)(lambda: rise(level, half).start())

        home_cross(order[0], 0).start()
        home_cross(order[1], 0).start()
        pass_on(order[0])
        home_cross(order[2], 0).start()
        pass_on(order[1])
        send_on(order[0])
        home_cross(order[3], 0).start()
        pass_on(order[2])
        send_on(order[1])
        pass_on(order[3])
        send_on(order[2])

        def finish(half, ref):
            slot = z * 2 + half
            total = gather(z, half)

            @pl.when(z == 0)
            def _():
                sink(z, half).wait_recv()
                ref[...] = (total + f32(from_above.at[slot])).astype(jnp.bfloat16)

            @pl.when(z == Z - 1)
            def _():
                rise(z, half).wait_recv()
                ref[...] = (total + f32(from_below.at[slot])).astype(jnp.bfloat16)

            @pl.when((z > 0) & (z < Z - 1))
            def _():
                sink(z, half).wait_recv()
                rise(z, half).wait_recv()
                ref[...] = (total + f32(from_above.at[slot]) + f32(from_below.at[slot])).astype(jnp.bfloat16)

        finish(1 - core, final)
        hand_over().start()
        finish(core, out)
        for level in order:
            for half in (0, 1):
                home_cross(level, half).wait_send()
                pl.when(level < z)(lambda: sink(level, half).wait_send())
                pl.when(level > z)(lambda: rise(level, half).wait_send())
        hand_over().wait_send()


def reduce_rows(term, block, tokens):
    dma = pltpu.SemaphoreType.DMA

    def pieces(count):
        return pltpu.VMEM((count, block, tokens), jnp.bfloat16)

    one = pltpu.VMEM((block, tokens), jnp.bfloat16)
    return pl.pallas_call(
        functools.partial(reduce_kernel, block),
        out_shape=jax.ShapeDtypeStruct((block, tokens), jnp.bfloat16),
        in_specs=[VMEM],
        out_specs=VMEM,
        scratch_shapes=[
            pieces(12), pieces(8), pieces(8), pieces(8), pieces(4), pieces(8), one, one,
            dma((12,)), dma((8,)), dma((8,)), dma((8,)), dma,
            dma((4,)), dma((4,)), dma((12,)), dma((8,)), dma,
        ],
        compiler_params=pltpu.CompilerParams(
            collective_id=1, has_side_effects=True, vmem_limit_bytes=VMEM_BYTES
        ),
    )(term)


def per_device_chips(n, hidden, head_weight, labels, loss_weight):
    tokens, block = hidden.shape
    features, logit_grad, token_loss = forward(
        hidden.T, head_weight, labels.reshape(1, tokens), loss_weight.reshape(1, tokens), n
    )
    term = lax.dot_general(
        head_weight, logit_grad, (((0,), (0,)), ((), ())), preferred_element_type=jnp.float32
    ).astype(jnp.bfloat16)
    hidden_grad = reduce_rows(term, block, tokens).T
    head_grad = lax.dot_general(
        logit_grad, features, (((1,), (1,)), ((), ())), preferred_element_type=jnp.float32
    ).astype(jnp.bfloat16)
    return hidden_grad, head_grad, token_loss.reshape(tokens)


def per_device(hidden, head_weight, labels, loss_weight):
    tokens = hidden.shape[0]
    rows = head_weight.shape[0]
    features = lax.all_gather(hidden, GROUP, axis=1, tiled=True)
    features = lax.all_to_all(features, "dp", split_axis=1, concat_axis=0, tiled=True)
    partial = lax.dot_general(
        head_weight, features, (((1,), (1,)), ((), ())), preferred_element_type=jnp.float32
    )
    logits = lax.psum_scatter(partial, "dp", scatter_dimension=1, tiled=True)
    entries = lax.axis_index(GROUP) * rows + jnp.arange(rows, dtype=jnp.int32)
    mask = (entries[:, None] == labels[None, :]).astype(jnp.float32)
    row_peak = lax.pmax(jnp.max(logits, axis=0), GROUP)
    shifted_exp = jnp.exp(logits - row_peak[None, :])
    row_total, picked = lax.psum((jnp.sum(shifted_exp, axis=0), jnp.sum(mask * logits, axis=0)), GROUP)
    token_loss = row_peak + jnp.log(row_total) - picked
    grad = (loss_weight[None, :] * (shifted_exp / row_total[None, :] - mask)).astype(jnp.bfloat16)
    grad = lax.all_gather(grad, "dp", axis=1, tiled=True)
    head_grad = jnp.dot(grad, features, preferred_element_type=jnp.float32).astype(jnp.bfloat16)
    term = lax.dot_general(grad, head_weight, (((0,), (0,)), ((), ())), preferred_element_type=jnp.float32)
    term = lax.all_to_all(term, "dp", split_axis=0, concat_axis=1, tiled=True)
    hidden_grad = lax.psum_scatter(term, GROUP, scatter_dimension=1, tiled=True).astype(jnp.bfloat16)
    return hidden_grad, head_grad, token_loss


def solution(mesh):
    sizes = dict(mesh.shape)
    if (sizes["pipe"], sizes["tensor"], sizes["dp"]) == (4, Z, 2):
        body = functools.partial(per_device_chips, 4 * Z)
    else:
        body = per_device
    return jax.shard_map(
        body,
        mesh=mesh,
        in_specs=(P("dp", GROUP), P(GROUP, "dp"), P("dp"), P("dp")),
        out_specs=(P("dp", GROUP), P(GROUP, "dp"), P("dp")),
        check_vma=False,
    )
```

profile of v0, /device:TPU:0, one launch (start us, length us, event | category | flops | bytes accessed | tf_op | source)
XLA Modules:
  0.0 94.4 jit_solution(4317224189655995350)
XLA Ops:
  0.6 0.0 copy-start
  0.6 0.9 copy-done
  1.5 0.0 copy-start.1
  1.5 0.7 copy-done.1
  2.2 0.0 copy-start.2
  2.2 0.7 copy-done.2
  2.9 0.0 slice-start
  2.9 47.2 %shard_map.67 = (bf16[2560,512]{1,0:T(8,128)(2,1)S(1)}, bf16[1187,512]{1,0:T(8,128)(2,1)S(1)}, f32[1,256]{1,0:T(1,128)S(1)}) custom-call(bf16[320,256]{1,0:T(8,128)(2,1)S(1)} %bitcast.12, bf16[1187,2560]{1,0:T(8,128)(2,1)} %weight.1, s32[1,256]{1,0:T(1,128)S(1)} %bitcast.13, f32[1,256]{1,0:T(1,128)S(1)} %bitcast.14), custom_call_target="tpu_custom_call" | custom-call | tf_op jit(solution)/shard_map/pallas_call | solution.py:316
  50.1 0.0 slice-start.1
  50.2 5.2 %convolution_convert_fusion = bf16[1187,2560]{1,0:T(8,128)(2,1)} fusion(bf16[1187,512]{1,0:T(8,128)(2,1)S(1)} %get-tuple-element.6, bf16[2560,512]{1,0:T(8,128)(2,1)S(1)} %get-tuple-element.7), kind=kOutput, calls=%fused_computation | convolution fusion | flops 3114688000 | bytes 9914368 | tf_op jit(solution)/shard_map/dot_general | solution.py:531
  55.4 0.0 slice-done
  55.4 0.0 slice-done.1
  55.4 3.9 %fusion.term = bf16[2560,512]{1,0:T(8,128)(2,1)S(1)} fusion(bf16[1187,512]{1,0:T(8,128)(2,1)S(1)} %get-tuple-element.6, bf16[1187,2560]{1,0:T(8,128)(2,1)S(1)} %bitcast.17), kind=kOutput, calls=%fused_computation.2 | convolution fusion | flops 3112960000 | bytes 9914368 | tf_op jit(solution)/shard_map/dot_general | solution.py:527
  59.3 33.9 %shard_map.68 = bf16[320,256]{1,0:T(8,128)(2,1)S(1)} custom-call(bf16[2560,512]{1,0:T(8,128)(2,1)S(1)} %fusion.term), custom_call_target="tpu_custom_call" | custom-call | tf_op jit(solution)/shard_map/pallas_call | solution.py:506
  93.2 0.7 copy.11
  93.9 0.6 copy.12
  (1 shorter events, 0.0 us)
Async XLA Ops:
  0.6 0.9 copy-start
  1.5 0.7 copy-start.1
  2.2 0.7 copy-start.2
  2.9 52.5 %slice-start = ((s8[6103040]{0:T(1024)(128)(4,1)}), s8[4194304]{0:T(1024)(128)(4,1)S(1)}, s32[]{:S(2)}) async-start(s8[6103040]{0:T(1024)(128)(4,1)} %bitcast.16), calls=%async_computation | async-start | bytes 8388608
  50.1 5.3 %slice-start.1 = ((s8[6103040]{0:T(1024)(128)(4,1)}), s8[1908736]{0:T(1024)(128)(4,1)S(1)}, s32[]{:S(2)}) async-start(s8[6103040]{0:T(1024)(128)(4,1)} %bitcast.16), calls=%async_computation.1 | async-start | bytes 3817472
where the time goes:
time: 94.6 us; the launch traced here: 94.4 us
  Pallas kernels  81.1 us (86%)
  matrix products  9.13 us (10%)
  local copies, waits for them, and re-layouts  3.51 us (4%)
    pallas_call x1, Pallas kernels, forward(): pl.pallas_call(functools.partial(forward_kernel, n, block), out_shape=(ja...  47.2 us
    pallas_call x1, Pallas kernels, reduce_rows(): pl.pallas_call(functools.partial(reduce_kernel, block), out_shape=jax.Sha...  33.9 us
    dot_general x1, matrix products, per_device_chips(): lax.dot_general(logit_grad, features, (((1,), (1,)), ((), ())), preferred...  5.24 us
    dot_general x1, matrix products, per_device_chips(): lax.dot_general(head_weight, logit_grad, (((0,), (0,)), ((), ())), prefer...  3.89 us
    unnamed x12, local copies, waits for them, and re-layouts  3.51 us

commit v1 on v0

--- a/solution.py
+++ b/solution.py
@@ -11,6 +11,7 @@
 MESH = pl.DeviceIdType.MESH
 VMEM = pl.BlockSpec(memory_space=pltpu.VMEM)
 ANY = pl.BlockSpec(memory_space=pl.ANY)
+HBM = pl.BlockSpec(memory_space=pltpu.HBM)
 VMEM_BYTES = 48 * 1024 * 1024
 Z = 4
 
@@ -57,12 +58,12 @@
     pl.semaphore_wait(barrier, n)
 
 
-def forward_kernel(
+def head_kernel(
     n, block, piece, weight, labels_in, loss_weight_in,
-    features_out, grad_out, loss_out,
-    features, weight_here, partial, partial_in, grad_here, stats, labels, loss_weight,
+    features_out, grad_out, loss_out, hidden_out,
+    features, weight_here, partial, partial_in, grads, term, stats, labels, loss_weight,
     recv, recv_low, send_up, send_down, low_up, low_down, send_x, send_y, send_y2, own_sem, weight_sem,
-    mate_sems, stat_send, stat_recv, out_sems, token_sems,
+    mate_sems, stat_send, stat_recv, out_sems, token_sems, *reduce_scratch
 ):
     me = Place()
     tokens = piece.shape[1]
@@ -115,7 +116,7 @@
         level = z + sign * distance
 
         def home():
-            for half in (0, 1):
+            for half in (core, 1 - core):
                 need(x, level, half, upper)
                 line_sends(level, half, sign, upper)
 
@@ -297,42 +298,79 @@
         where = pl.ds(start, size)
         share = jnp.exp(partial_in[where] - row_peak) * inverse
         hit = jnp.where(is_target(start, size), 1.0, 0.0)
-        grad_here[where] = (scale * (share - hit)).astype(jnp.bfloat16)
-    mine = grad_out.at[:, pl.ds(pl.multiple_of(core * tokens, tokens), tokens)]
-    keep = pltpu.make_async_copy(grad_here, mine, out_sems.at[1])
-    share_grad = remote(grad_here, mine, mate_sems.at[2], mate_sems.at[3], me.mate)
+        grads[core, where] = (scale * (share - hit)).astype(jnp.bfloat16)
+    share_grad = remote(grads.at[core], grads.at[core], mate_sems.at[2], mate_sems.at[3], me.mate)
     share_grad.start()
-    keep.start()
+
+    def keep(half, sem):
+        there = grad_out.at[:, pl.ds(pl.multiple_of(half * tokens, tokens), tokens)]
+        return pltpu.make_async_copy(grads.at[half], there, sem)
+
+    keep(core, out_sems.at[1]).start()
+
+    def multiply_back(pair, half):
+        width = 2 * block
+        depth = pl.ds(pl.multiple_of(pair * width, width), width)
+        term[depth, pl.ds(pl.multiple_of(half * tokens, tokens), tokens)] = lax.dot_general(
+            weight_here[:, depth], grads[half], (((0,), (0,)), ((), ())), preferred_element_type=jnp.float32
+        ).astype(jnp.bfloat16)
+
+    def back(step, carry):
+        multiply_back(jnp.where(step % 2 == 0, far, near), jnp.where(step < 2, core, 1 - core))
+        return carry
+
+    def back_rest(step, carry):
+        column = jnp.where(step % 2 == 0, 1 - x, x)
+        multiply_back(column * 2 + z // 2, step // 2)
+        return carry
+
+    lax.fori_loop(0, 2, back, 0)
+    share_grad.wait_recv()
+    keep(1 - core, out_sems.at[2]).start()
+    lax.fori_loop(2, 4, back, 0)
+    reduce_rows(me, block, term, hidden_out, lambda: lax.fori_loop(0, 4, back_rest, 0), *reduce_scratch)
+
     lax.fori_loop(1, n, wait_stat_send, 0)
-    keep.wait()
-    share_grad.wait()
+    share_grad.wait_send()
+    keep(core, out_sems.at[1]).wait()
+    keep(1 - core, out_sems.at[2]).wait()
     store_features.wait()
 
 
-def forward(hidden_t, head_weight, labels, loss_weight, n):
+def head(hidden_t, head_weight, labels, loss_weight, n):
     block, tokens = hidden_t.shape
     rows, width = head_weight.shape
     dma = pltpu.SemaphoreType.DMA
+
+    def pieces(count):
+        return pltpu.VMEM((count, block, tokens), jnp.bfloat16)
+
+    one = pltpu.VMEM((block, tokens), jnp.bfloat16)
     return pl.pallas_call(
-        functools.partial(forward_kernel, n, block),
+        functools.partial(head_kernel, n, block),
         out_shape=(
             jax.ShapeDtypeStruct((width, 2 * tokens), jnp.bfloat16),
             jax.ShapeDtypeStruct((rows, 2 * tokens), jnp.bfloat16),
             jax.ShapeDtypeStruct((1, tokens), jnp.float32),
+            jax.ShapeDtypeStruct((block, tokens), jnp.bfloat16),
         ),
-        in_specs=[ANY, ANY, ANY, ANY],
-        out_specs=(ANY, ANY, VMEM),
+        in_specs=[HBM, ANY, HBM, HBM],
+        out_specs=(ANY, ANY, VMEM, VMEM),
         scratch_shapes=[
             pltpu.VMEM((width, 2 * tokens), jnp.bfloat16),
             pltpu.VMEM((rows, width), jnp.bfloat16),
             pltpu.VMEM((2, rows, tokens), jnp.float32),
             pltpu.VMEM((rows, tokens), jnp.float32),
-            pltpu.VMEM((rows, tokens), jnp.bfloat16),
+            pltpu.VMEM((2, rows, tokens), jnp.bfloat16),
+            pltpu.VMEM((width, 2 * tokens), jnp.bfloat16),
             pltpu.VMEM((n, 8, tokens), jnp.float32),
             pltpu.VMEM((1, tokens), jnp.int32),
             pltpu.VMEM((1, tokens), jnp.float32),
             dma((16,)), dma((16,)), dma((8,)), dma((8,)), dma((16,)), dma((16,)), dma((8,)), dma((8,)), dma((4,)),
-            dma, dma, dma((4,)), dma((n,)), dma((n,)), dma((2,)), dma((2,)),
+            dma, dma, dma((4,)), dma((n,)), dma((n,)), dma((3,)), dma((2,)),
+            pieces(12), pieces(8), pieces(8), pieces(8), pieces(4), pieces(8), one, one,
+            dma((12,)), dma((8,)), dma((8,)), dma((8,)), dma,
+            dma((4,)), dma((4,)), dma((12,)), dma((8,)), dma,
         ],
         compiler_params=pltpu.CompilerParams(
             collective_id=0, has_side_effects=True, vmem_limit_bytes=VMEM_BYTES
@@ -340,28 +378,14 @@
     )(hidden_t, head_weight, labels, loss_weight)
 
 
-def reduce_kernel(
-    block, term, out,
+def reduce_rows(
+    me, block, term, out, finish_term,
     from_y, from_x, from_below, from_above, passed, summed, final, landed,
     recv_y, recv_x, recv_below, recv_above, recv_final,
     send_x, send_pass, send_y, send_z, send_final,
 ):
-    me = Place()
     tokens = out.shape[1]
     x, z, core = me.x, me.z, me.core
-    barrier = pltpu.get_barrier_semaphore()
-    for peer in (me.x_peer, me.y_peer, me.mate):
-        pl.semaphore_signal(barrier, inc=1, device_id=peer, device_id_type=MESH)
-
-    @pl.when(z > 0)
-    def _():
-        pl.semaphore_signal(barrier, inc=1, device_id=me.down, device_id_type=MESH)
-
-    @pl.when(z < Z - 1)
-    def _():
-        pl.semaphore_signal(barrier, inc=1, device_id=me.up, device_id_type=MESH)
-
-    pl.semaphore_wait(barrier, 3 + (z + Z - 1) // Z + (2 * (Z - 1) - z) // Z)
 
     def own(column, level, half):
         start = pl.multiple_of((column * Z + level) * block, block)
@@ -403,16 +427,28 @@
 
     @pl.when(me.away)
     def _():
-        away_cross(order[0]).start()
-        away_diagonal(order[0]).start()
+        for level in order[:2]:
+            away_cross(level).start()
+            away_diagonal(level).start()
+            away_line(level, 1).start()
+
+    @pl.when(me.home)
+    def _():
+        for level in order[:2]:
+            home_cross(level, 0).start()
+
+    finish_term()
+
+    @pl.when(me.away)
+    def _():
         for at, level in enumerate(order):
-            away_line(level, 1).start()
-            if at + 1 < Z:
-                away_cross(order[at + 1]).start()
-                away_diagonal(order[at + 1]).start()
             away_cross(level).wait_recv()
             passed[level] = (f32(own(x, level, 0)) + f32(from_x.at[level * 2])).astype(jnp.bfloat16)
             away_line(level, 0).start()
+            if at + 2 < Z:
+                away_cross(order[at + 2]).start()
+                away_diagonal(order[at + 2]).start()
+                away_line(order[at + 2], 1).start()
         for level in order:
             away_cross(level).wait_send()
             away_diagonal(level).wait_send()
@@ -453,8 +489,6 @@
                 pl.when(level < z)(lambda: sink(level, half).start())
                 pl.when(level > z)(lambda: rise(level, half).start())
 
-        home_cross(order[0], 0).start()
-        home_cross(order[1], 0).start()
         pass_on(order[0])
         home_cross(order[2], 0).start()
         pass_on(order[1])
@@ -496,42 +530,15 @@
         hand_over().wait_send()
 
 
-def reduce_rows(term, block, tokens):
-    dma = pltpu.SemaphoreType.DMA
-
-    def pieces(count):
-        return pltpu.VMEM((count, block, tokens), jnp.bfloat16)
-
-    one = pltpu.VMEM((block, tokens), jnp.bfloat16)
-    return pl.pallas_call(
-        functools.partial(reduce_kernel, block),
-        out_shape=jax.ShapeDtypeStruct((block, tokens), jnp.bfloat16),
-        in_specs=[VMEM],
-        out_specs=VMEM,
-        scratch_shapes=[
-            pieces(12), pieces(8), pieces(8), pieces(8), pieces(4), pieces(8), one, one,
-            dma((12,)), dma((8,)), dma((8,)), dma((8,)), dma,
-            dma((4,)), dma((4,)), dma((12,)), dma((8,)), dma,
-        ],
-        compiler_params=pltpu.CompilerParams(
-            collective_id=1, has_side_effects=True, vmem_limit_bytes=VMEM_BYTES
-        ),
-    )(term)
-
-
 def per_device_chips(n, hidden, head_weight, labels, loss_weight):
     tokens, block = hidden.shape
-    features, logit_grad, token_loss = forward(
+    features, logit_grad, token_loss, hidden_grad = head(
         hidden.T, head_weight, labels.reshape(1, tokens), loss_weight.reshape(1, tokens), n
     )
-    term = lax.dot_general(
-        head_weight, logit_grad, (((0,), (0,)), ((), ())), preferred_element_type=jnp.float32
-    ).astype(jnp.bfloat16)
-    hidden_grad = reduce_rows(term, block, tokens).T
     head_grad = lax.dot_general(
         logit_grad, features, (((1,), (1,)), ((), ())), preferred_element_type=jnp.float32
     ).astype(jnp.bfloat16)
-    return hidden_grad, head_grad, token_loss.reshape(tokens)
+    return hidden_grad.T, head_grad, token_loss.reshape(tokens)
 
 
 def per_device(hidden, head_weight, labels, loss_weight):

time: 94.6 us -> 90 us (0.951)
  matrix products: 9.13 us -> 5.24 us
    dot_general x1 -> x0, matrix products: 3.89 us -> none  [per_device_chips(): lax.dot_general(head_weight, logit_grad, (((0,), (0,)), ((), ())), prefer...]
    pallas_call x2 -> x1, Pallas kernels: 81.1 us -> 80.5 us  [head(): pl.pallas_call(functools.partial(head_kernel, n, block), out_shape=(jax.S...]
    unnamed x12 -> x8, local copies, waits for them, and re-layouts: 3.51 us -> 3.49 us
where the time goes in v1:
time: 90 us; the launch traced here: 89.9 us
  Pallas kernels  80.5 us (89%)
  matrix products  5.24 us (6%)
  local copies, waits for them, and re-layouts  3.49 us (4%)
    pallas_call x1, Pallas kernels, head(): pl.pallas_call(functools.partial(head_kernel, n, block), out_shape=(jax.S...  80.5 us
    dot_general x1, matrix products, per_device_chips(): lax.dot_general(logit_grad, features, (((1,), (1,)), ((), ())), preferred...  5.24 us
    unnamed x8, local copies, waits for them, and re-layouts  3.49 us

profile of v1, /device:TPU:0, one launch (start us, length us, event | category | flops | bytes accessed | tf_op | source)
XLA Modules:
  0.0 89.9 jit_solution(13151975464951619451)
XLA Ops:
  0.6 0.0 copy-start
  0.6 0.9 %copy-done = bf16[256,320]{0,1:T(8,128)(2,1)S(1)} copy-done((bf16[256,320]{0,1:T(8,128)(2,1)S(1)}, bf16[256,320]{0,1:T(8,128)(2,1)}, u32[]{:S(2)}) %copy-start) | copy-done | bytes 163864
  1.5 0.0 copy-start.1
  1.6 0.7 copy-done.1
  2.2 0.0 copy-start.2
  2.2 0.7 copy-done.2
  2.9 80.5 %shard_map.67 = (bf16[2560,512]{1,0:T(8,128)(2,1)S(1)}, bf16[1187,512]{1,0:T(8,128)(2,1)S(1)}, f32[1,256]{1,0:T(1,128)S(1)}, bf16[320,256]{1,0:T(8,128)(2,1)S(1)}) custom-call(bf16[320,256]{1,0:T(8,128)(2,1)S(1)} %bitcast.7, bf16[1187,2560]{1,0:T(8,128)(2,1)} %weight.1, s32[1,256]{1,0:T(1,128)S(1)} %bitcast.9, f32[1,256]{1,0:T(1,128)S(1)} %bitcast.10), custom_call_target="tpu_custom_call" | custom-call | tf_op jit(solution)/shard_map/pallas_call | solution.py:349
  83.4 5.2 %convolution_convert_fusion = bf16[1187,2560]{1,0:T(8,128)(2,1)} fusion(bf16[1187,512]{1,0:T(8,128)(2,1)S(1)} %get-tuple-element.8, bf16[2560,512]{1,0:T(8,128)(2,1)S(1)} %get-tuple-element.9), kind=kOutput, calls=%fused_computation | convolution fusion | flops 3114688000 | bytes 9914368 | tf_op jit(solution)/shard_map/dot_general | solution.py:538
  88.6 0.7 copy.9
  89.3 0.6 copy.10
Async XLA Ops:
  0.6 0.9 %copy-start = (bf16[256,320]{0,1:T(8,128)(2,1)S(1)}, bf16[256,320]{0,1:T(8,128)(2,1)}, u32[]{:S(2)}) copy-start(bf16[256,320]{0,1:T(8,128)(2,1)} %param.4) | copy-start | bytes 491524
  1.5 0.7 copy-start.1
  2.2 0.7 copy-start.2

commit v2 on v1

--- a/solution.py
+++ b/solution.py
@@ -31,8 +31,6 @@
         self.away = self.y == 1 - self.core
         self.x_peer = {"pipe": self.y * 2 + 1 - self.x}
         self.y_peer = {"pipe": (1 - self.y) * 2 + self.x}
-        self.up = {"tensor": self.z + 1}
-        self.down = {"tensor": self.z - 1}
         self.mate = {"dp": 1 - self.core}
 
 
@@ -62,8 +60,8 @@
     n, block, piece, weight, labels_in, loss_weight_in,
     features_out, grad_out, loss_out, hidden_out,
     features, weight_here, partial, partial_in, grads, term, stats, labels, loss_weight,
-    recv, recv_low, send_up, send_down, low_up, low_down, send_x, send_y, send_y2, own_sem, weight_sem,
-    mate_sems, stat_send, stat_recv, out_sems, token_sems, *reduce_scratch
+    recv, send_z, send_x, send_y, send_y2, own_sem, weight_sem,
+    swap_send, swap_recv, mate_sems, stat_send, stat_recv, out_sems, token_sems, *reduce_scratch
 ):
     me = Place()
     tokens = piece.shape[1]
@@ -78,20 +76,14 @@
     for load in load_tokens:
         load.start()
     greet_group(me, n)
-    low = block // 80 * 16
-    whole, upper, lower = (0, block), (low, block - low), (0, low)
-
-    def at(column, level, half, part):
-        start = pl.multiple_of((column * Z + level) * block + part[0], 16)
-        return features.at[pl.ds(start, part[1]), pl.ds(pl.multiple_of(half * tokens, tokens), tokens)]
-
-    def copy(column, level, half, send_sem, device, part):
-        here = at(column, level, half, part)
-        sems = recv_low if part is lower else recv
-        return remote(here, here, send_sem, sems.at[(column * Z + level) * 2 + half], device)
-
-    def arrived(column, level, half, part):
-        copy(column, level, half, send_y.at[0], me.mate, part).wait_recv()
+
+    def at(column, level, half):
+        start = pl.multiple_of((column * Z + level) * block, block)
+        return features.at[pl.ds(start, block), pl.ds(pl.multiple_of(half * tokens, tokens), tokens)]
+
+    def copy(column, level, half, send_sem, device):
+        here = at(column, level, half)
+        return remote(here, here, send_sem, recv.at[(column * Z + level) * 2 + half], device)
 
     def run(transfer):
         if waiting:
@@ -99,31 +91,33 @@
         else:
             transfer.start()
 
-    def need(column, level, half, part):
+    def need(column, level, half):
         if not waiting:
-            arrived(column, level, half, part)
-
-    def line_sends(level, half, sign, part):
+            copy(column, level, half, send_y.at[0], me.mate).wait_recv()
+
+    def line_sends(level, half):
         slot = level * 2 + half
-        if sign <= 0:
-            pl.when(z < Z - 1)(lambda: run(copy(x, level, half, send_up.at[slot], me.up, upper)))
-        if sign >= 0:
-            pl.when(z > 0)(lambda: run(copy(x, level, half, send_down.at[slot], me.down, upper)))
-        run(copy(x, level, half, send_x.at[slot], me.x_peer, part))
-        run(copy(x, level, half, send_y.at[slot], me.y_peer, part))
+        run(copy(x, level, half, send_x.at[slot], me.x_peer))
+        run(copy(x, level, half, send_y.at[slot], me.y_peer))
+
+    def own_sends(half):
+        for step in range(1, Z):
+            other = (z + step) % Z
+            run(copy(x, z, half, send_z.at[other * 2 + half], {"tensor": other}))
+        line_sends(z, half)
 
     def line_step(distance, sign):
         level = z + sign * distance
 
         def home():
             for half in (core, 1 - core):
-                need(x, level, half, upper)
-                line_sends(level, half, sign, upper)
+                need(x, level, half)
+                line_sends(level, half)
 
         def away():
-            need(x, level, 0, upper)
-            run(copy(x, level, 0, send_x.at[level * 2], me.x_peer, upper))
-            need(x, level, 1, upper)
+            need(x, level, 0)
+            run(copy(x, level, 0, send_x.at[level * 2], me.x_peer))
+            need(x, level, 1)
 
         valid = (level >= 0) & (level < Z)
         pl.when(valid & me.home)(home)
@@ -132,129 +126,107 @@
     def first_step():
         @pl.when(me.home)
         def _():
-            line_sends(z, core, 0, whole)
-            need(x, z, 1 - core, whole)
-            line_sends(z, 1 - core, 0, whole)
+            own_sends(core)
+            need(x, z, 1 - core)
+            own_sends(1 - core)
 
         @pl.when(me.away)
         def _():
-            need(x, z, 0, whole)
-            run(copy(x, z, 0, send_x.at[z * 2], me.x_peer, whole))
-            need(x, z, 1, whole)
+            need(x, z, 0)
+            run(copy(x, z, 0, send_x.at[z * 2], me.x_peer))
+            need(x, z, 1)
 
     def peer_step(distance, sign):
         level = z + sign * distance
-        part = upper if distance else whole
-        valid = (level >= 0) & (level < Z)
-        if not waiting:
-            @pl.when(valid)
-            def _():
-                arrived(1 - x, level, 0, part)
-                arrived(1 - x, level, 1, part)
-
-        pl.when(valid & me.home)(
-            lambda: run(copy(1 - x, level, 1, send_y2.at[level], me.y_peer, part))
-        )
-
-    def low_step(distance, sign):
-        level = z + sign * distance
-
-        def each(which, carry):
-            column, half = which // 2, which % 2
-            slot = (column * Z + level) * 2 + half
-            if distance:
-                need(column, level, half, lower)
-            if sign <= 0:
-                pl.when(z < Z - 1)(lambda: run(copy(column, level, half, low_up.at[slot], me.up, lower)))
-            if sign >= 0:
-                pl.when(z > 0)(lambda: run(copy(column, level, half, low_down.at[slot], me.down, lower)))
-            return carry
 
         @pl.when((level >= 0) & (level < Z))
         def _():
-            lax.fori_loop(0, 4, each, 0)
-
-    def multiply(pair, half, first):
+            need(1 - x, level, 1)
+            pl.when(me.home)(lambda: run(copy(1 - x, level, 1, send_y2.at[level], me.y_peer)))
+            need(1 - x, level, 0)
+
+    cuts = spans(rows, 608)
+
+    def multiply(pair, half, first, cut):
         width = 2 * block
         depth = pl.ds(pl.multiple_of(pair * width, width), width)
         right = features[depth, pl.ds(pl.multiple_of(half * tokens, tokens), tokens)]
-        for start, size in spans(rows, 592):
-            part = jnp.dot(weight_here[pl.ds(start, size), depth], right, preferred_element_type=jnp.float32)
-            where = (half, pl.ds(start, size))
-            partial[where] = part if first else partial[where] + part
+        part = jnp.dot(weight_here[pl.ds(*cut), depth], right, preferred_element_type=jnp.float32)
+        where = (half, pl.ds(*cut))
+        partial[where] = part if first else partial[where] + part
 
     def multiply_both(pair, first=False):
         def step(half, carry):
-            multiply(pair, half, first)
+            for cut in cuts:
+                multiply(pair, half, first, cut)
             return carry
 
         lax.fori_loop(0, 2, step, 0)
 
     waiting = False
-    mine = at(x, z, core, whole)
+    mine = at(x, z, core)
     own_copy = pltpu.make_async_copy(piece, mine, own_sem)
     own_send = remote(piece, mine, own_sem, recv.at[(x * Z + z) * 2 + core], me.mate)
     pl.when(me.home)(own_copy.start)
     pl.when(me.away)(own_send.start)
     pl.when(me.home)(own_copy.wait)
+    near, far = x * 2 + 1 - z // 2, (1 - x) * 2 + 1 - z // 2
+
+    def both(step, distance):
+        for sign in (-1, 1):
+            step(distance, sign)
+
     first_step()
-    for sign in (-1, 1):
-        line_step(1, sign)
+    both(line_step, 1)
     peer_step(0, 1)
-    low_step(0, 0)
-    for sign in (-1, 1):
-        line_step(2, sign)
-    for sign in (-1, 1):
-        peer_step(1, sign)
-    for sign in (-1, 1):
-        low_step(1, sign)
+    both(line_step, 2)
+    both(line_step, 3)
     load_weight.wait()
     multiply_both(x * 2 + z // 2, True)
-    for sign in (-1, 1):
-        line_step(3, sign)
-    for sign in (-1, 1):
-        peer_step(2, sign)
-    for sign in (-1, 1):
-        low_step(2, sign)
+    both(peer_step, 1)
+    multiply_both(near)
+    both(peer_step, 2)
     multiply_both((1 - x) * 2 + z // 2)
-    for sign in (-1, 1):
-        peer_step(3, sign)
-    for sign in (-1, 1):
-        low_step(3, sign)
+    both(peer_step, 3)
     store_features = pltpu.make_async_copy(features, features_out, out_sems.at[0])
     store_features.start()
-    near, far = x * 2 + 1 - z // 2, (1 - x) * 2 + 1 - z // 2
-    multiply(near, 1 - core, False)
-    multiply(far, 1 - core, False)
-    swap = remote(partial.at[1 - core], partial_in, mate_sems.at[0], mate_sems.at[1], me.mate)
-    swap.start()
-    multiply(near, core, False)
-    multiply(far, core, False)
+    swaps = []
+    for at_cut, (start, size) in enumerate(cuts):
+        multiply(far, 1 - core, False, (start, size))
+        sent = pl.ds(start, -(-size // 8) * 8)
+        swaps.append(remote(
+            partial.at[1 - core, sent], partial_in.at[sent],
+            swap_send.at[at_cut], swap_recv.at[at_cut], me.mate,
+        ))
+        swaps[-1].start()
+    for cut in cuts:
+        multiply(far, core, False, cut)
 
     waiting = True
     pl.when(me.away)(own_send.wait_send)
     first_step()
     peer_step(0, 1)
-    low_step(0, 0)
     for distance in (1, 2, 3):
-        for sign in (-1, 1):
-            line_step(distance, sign)
-            peer_step(distance, sign)
-            low_step(distance, sign)
+        both(line_step, distance)
+        both(peer_step, distance)
     for load in load_tokens:
         load.wait()
-    swap.wait()
 
     index = me.pipe * Z + z
     target = labels[...] - index * rows
     peak = jnp.full((1, tokens), -jnp.inf, jnp.float32)
     picked = jnp.zeros((1, tokens), jnp.float32)
-    parts = spans(rows, 128)
+    parts = [
+        (cut + start, size) for cut, length in cuts for start, size in spans(length, 128)
+    ]
 
     def is_target(start, size):
         return lax.broadcasted_iota(jnp.int32, (size, tokens), 0) + start == target
 
     for start, size in parts:
+        for swap, cut in zip(swaps, cuts):
+            if start == cut[0]:
+                swap.wait_recv()
         where = pl.ds(start, size)
         logits = partial[core, where] + partial_in[where]
         partial_in[where] = logits
@@ -299,7 +271,7 @@
         share = jnp.exp(partial_in[where] - row_peak) * inverse
         hit = jnp.where(is_target(start, size), 1.0, 0.0)
         grads[core, where] = (scale * (share - hit)).astype(jnp.bfloat16)
-    share_grad = remote(grads.at[core], grads.at[core], mate_sems.at[2], mate_sems.at[3], me.mate)
+    share_grad = remote(grads.at[core], grads.at[core], mate_sems.at[0], mate_sems.at[1], me.mate)
     share_grad.start()
 
     def keep(half, sem):
@@ -331,6 +303,8 @@
     reduce_rows(me, block, term, hidden_out, lambda: lax.fori_loop(0, 4, back_rest, 0), *reduce_scratch)
 
     lax.fori_loop(1, n, wait_stat_send, 0)
+    for swap in swaps:
+        swap.wait_send()
     share_grad.wait_send()
     keep(core, out_sems.at[1]).wait()
     keep(1 - core, out_sems.at[2]).wait()
@@ -340,6 +314,7 @@
 def head(hidden_t, head_weight, labels, loss_weight, n):
     block, tokens = hidden_t.shape
     rows, width = head_weight.shape
+    padded = -(-rows // 8) * 8
     dma = pltpu.SemaphoreType.DMA
 
     def pieces(count):
@@ -359,17 +334,17 @@
         scratch_shapes=[
             pltpu.VMEM((width, 2 * tokens), jnp.bfloat16),
             pltpu.VMEM((rows, width), jnp.bfloat16),
-            pltpu.VMEM((2, rows, tokens), jnp.float32),
-            pltpu.VMEM((rows, tokens), jnp.float32),
+            pltpu.VMEM((2, padded, tokens), jnp.float32),
+            pltpu.VMEM((padded, tokens), jnp.float32),
             pltpu.VMEM((2, rows, tokens), jnp.bfloat16),
             pltpu.VMEM((width, 2 * tokens), jnp.bfloat16),
             pltpu.VMEM((n, 8, tokens), jnp.float32),
             pltpu.VMEM((1, tokens), jnp.int32),
             pltpu.VMEM((1, tokens), jnp.float32),
-            dma((16,)), dma((16,)), dma((8,)), dma((8,)), dma((16,)), dma((16,)), dma((8,)), dma((8,)), dma((4,)),
-            dma, dma, dma((4,)), dma((n,)), dma((n,)), dma((3,)), dma((2,)),
-            pieces(12), pieces(8), pieces(8), pieces(8), pieces(4), pieces(8), one, one,
-            dma((12,)), dma((8,)), dma((8,)), dma((8,)), dma,
+            dma((16,)), dma((8,)), dma((8,)), dma((8,)), dma((4,)), dma, dma,
+            dma((2,)), dma((2,)), dma((2,)), dma((n,)), dma((n,)), dma((3,)), dma((2,)),
+            pieces(12), pieces(8), pieces(8), pieces(4), pieces(8), one, one,
+            dma((12,)), dma((8,)), dma((8,)), dma,
             dma((4,)), dma((4,)), dma((12,)), dma((8,)), dma,
         ],
         compiler_params=pltpu.CompilerParams(
@@ -380,8 +355,8 @@
 
 def reduce_rows(
     me, block, term, out, finish_term,
-    from_y, from_x, from_below, from_above, passed, summed, final, landed,
-    recv_y, recv_x, recv_below, recv_above, recv_final,
+    from_y, from_x, from_z, passed, summed, final, landed,
+    recv_y, recv_x, recv_z, recv_final,
     send_x, send_pass, send_y, send_z, send_final,
 ):
     tokens = out.shape[1]
@@ -411,13 +386,11 @@
         sem = send_pass.at[level] if half else send_x.at[level]
         return remote(source, from_x.at[slot], sem, recv_x.at[slot], me.x_peer)
 
-    def rise(level, half):
-        slot = level * 2 + half
-        return remote(summed.at[slot], from_below.at[slot], send_z.at[slot], recv_below.at[slot], me.up)
-
-    def sink(level, half):
-        slot = level * 2 + half
-        return remote(summed.at[slot], from_above.at[slot], send_z.at[slot], recv_above.at[slot], me.down)
+    def along(level, half):
+        slot, source = level * 2 + half, z * 2 + half
+        return remote(
+            summed.at[slot], from_z.at[source], send_z.at[slot], recv_z.at[source], {"tensor": level}
+        )
 
     def hand_over():
         return remote(final, landed, send_final, recv_final, me.mate)
@@ -472,22 +445,8 @@
 
         def send_on(level):
             for half in (1, 0):
-                slot = level * 2 + half
-                total = gather(level, half)
-                summed[slot] = total.astype(jnp.bfloat16)
-
-                @pl.when((level < z) & (z < Z - 1))
-                def _():
-                    sink(level, half).wait_recv()
-                    summed[slot] = (total + f32(from_above.at[slot])).astype(jnp.bfloat16)
-
-                @pl.when((level > z) & (z > 0))
-                def _():
-                    rise(level, half).wait_recv()
-                    summed[slot] = (total + f32(from_below.at[slot])).astype(jnp.bfloat16)
-
-                pl.when(level < z)(lambda: sink(level, half).start())
-                pl.when(level > z)(lambda: rise(level, half).start())
+                summed[level * 2 + half] = gather(level, half).astype(jnp.bfloat16)
+                along(level, half).start()
 
         pass_on(order[0])
         home_cross(order[2], 0).start()
@@ -500,24 +459,12 @@
         send_on(order[2])
 
         def finish(half, ref):
-            slot = z * 2 + half
             total = gather(z, half)
-
-            @pl.when(z == 0)
-            def _():
-                sink(z, half).wait_recv()
-                ref[...] = (total + f32(from_above.at[slot])).astype(jnp.bfloat16)
-
-            @pl.when(z == Z - 1)
-            def _():
-                rise(z, half).wait_recv()
-                ref[...] = (total + f32(from_below.at[slot])).astype(jnp.bfloat16)
-
-            @pl.when((z > 0) & (z < Z - 1))
-            def _():
-                sink(z, half).wait_recv()
-                rise(z, half).wait_recv()
-                ref[...] = (total + f32(from_above.at[slot]) + f32(from_below.at[slot])).astype(jnp.bfloat16)
+            for step in range(1, Z):
+                slot = (z + step) % Z * 2 + half
+                remote(final, from_z.at[slot], send_final, recv_z.at[slot], me.mate).wait_recv()
+                total += f32(from_z.at[slot])
+            ref[...] = total.astype(jnp.bfloat16)
 
         finish(1 - core, final)
         hand_over().start()
@@ -525,8 +472,9 @@
         for level in order:
             for half in (0, 1):
                 home_cross(level, half).wait_send()
-                pl.when(level < z)(lambda: sink(level, half).wait_send())
-                pl.when(level > z)(lambda: rise(level, half).wait_send())
+        for level in order[:3]:
+            for half in (0, 1):
+                along(level, half).wait_send()
         hand_over().wait_send()
 
 

time: 90 us -> 93.8 us (1.042)
  Pallas kernels: 80.5 us -> 84.2 us
    pallas_call x1, Pallas kernels: 80.5 us -> 84.2 us  [head(): pl.pallas_call(functools.partial(head_kernel, n, block), out_shape=(jax.S...]
where the time goes in v2:
time: 93.8 us; the launch traced here: 93.6 us
  Pallas kernels  84.2 us (90%)
  matrix products  5.24 us (6%)
  local copies, waits for them, and re-layouts  3.49 us (4%)
    pallas_call x1, Pallas kernels, head(): pl.pallas_call(functools.partial(head_kernel, n, block), out_shape=(jax.S...  84.2 us
    dot_general x1, matrix products, per_device_chips(): lax.dot_general(logit_grad, features, (((1,), (1,)), ((), ())), preferred...  5.24 us
    unnamed x8, local copies, waits for them, and re-layouts  3.49 us

profile of v2, /device:TPU:0, one launch (start us, length us, event | category | flops | bytes accessed | tf_op | source)
XLA Modules:
  0.0 93.6 jit_solution(17723077986741113978)
XLA Ops:
  0.6 0.0 copy-start
  0.6 0.9 copy-done
  1.5 0.0 copy-start.1
  1.6 0.7 copy-done.1
  2.2 0.0 copy-start.2
  2.2 0.7 copy-done.2
  2.9 84.2 %shard_map.67 = (bf16[2560,512]{1,0:T(8,128)(2,1)S(1)}, bf16[1187,512]{1,0:T(8,128)(2,1)S(1)}, f32[1,256]{1,0:T(1,128)S(1)}, bf16[320,256]{1,0:T(8,128)(2,1)S(1)}) custom-call(bf16[320,256]{1,0:T(8,128)(2,1)S(1)} %bitcast.7, bf16[1187,2560]{1,0:T(8,128)(2,1)} %weight.1, s32[1,256]{1,0:T(1,128)S(1)} %bitcast.9, f32[1,256]{1,0:T(1,128)S(1)} %bitcast.10), custom_call_target="tpu_custom_call" | custom-call | tf_op jit(solution)/shard_map/pallas_call | solution.py:324
  87.1 5.2 %convolution_convert_fusion = bf16[1187,2560]{1,0:T(8,128)(2,1)} fusion(bf16[1187,512]{1,0:T(8,128)(2,1)S(1)} %get-tuple-element.8, bf16[2560,512]{1,0:T(8,128)(2,1)S(1)} %get-tuple-element.9), kind=kOutput, calls=%fused_computation | convolution fusion | flops 3114688000 | bytes 9914368 | tf_op jit(solution)/shard_map/dot_general | solution.py:486
  92.4 0.7 copy.9
  93.0 0.6 copy.10
Async XLA Ops:
  0.6 0.9 copy-start
  1.5 0.7 copy-start.1
  2.2 0.7 copy-start.2

commit v3 on v1

--- a/solution.py
+++ b/solution.py
@@ -63,7 +63,7 @@
     features_out, grad_out, loss_out, hidden_out,
     features, weight_here, partial, partial_in, grads, term, stats, labels, loss_weight,
     recv, recv_low, send_up, send_down, low_up, low_down, send_x, send_y, send_y2, own_sem, weight_sem,
-    mate_sems, stat_send, stat_recv, out_sems, token_sems, *reduce_scratch
+    swap_send, swap_recv, mate_sems, stat_send, stat_recv, out_sems, token_sems, *reduce_scratch
 ):
     me = Place()
     tokens = piece.shape[1]
@@ -174,18 +174,20 @@
         def _():
             lax.fori_loop(0, 4, each, 0)
 
-    def multiply(pair, half, first):
+    cuts = spans(rows, 608)
+
+    def multiply(pair, half, first, cut):
         width = 2 * block
         depth = pl.ds(pl.multiple_of(pair * width, width), width)
         right = features[depth, pl.ds(pl.multiple_of(half * tokens, tokens), tokens)]
-        for start, size in spans(rows, 592):
-            part = jnp.dot(weight_here[pl.ds(start, size), depth], right, preferred_element_type=jnp.float32)
-            where = (half, pl.ds(start, size))
-            partial[where] = part if first else partial[where] + part
+        part = jnp.dot(weight_here[pl.ds(*cut), depth], right, preferred_element_type=jnp.float32)
+        where = (half, pl.ds(*cut))
+        partial[where] = part if first else partial[where] + part
 
     def multiply_both(pair, first=False):
         def step(half, carry):
-            multiply(pair, half, first)
+            for cut in cuts:
+                multiply(pair, half, first, cut)
             return carry
 
         lax.fori_loop(0, 2, step, 0)
@@ -224,12 +226,19 @@
     store_features = pltpu.make_async_copy(features, features_out, out_sems.at[0])
     store_features.start()
     near, far = x * 2 + 1 - z // 2, (1 - x) * 2 + 1 - z // 2
-    multiply(near, 1 - core, False)
-    multiply(far, 1 - core, False)
-    swap = remote(partial.at[1 - core], partial_in, mate_sems.at[0], mate_sems.at[1], me.mate)
-    swap.start()
-    multiply(near, core, False)
-    multiply(far, core, False)
+    swaps = []
+    for at_cut, (start, size) in enumerate(cuts):
+        multiply(near, 1 - core, False, (start, size))
+        multiply(far, 1 - core, False, (start, size))
+        sent = pl.ds(start, -(-size // 8) * 8)
+        swaps.append(remote(
+            partial.at[1 - core, sent], partial_in.at[sent],
+            swap_send.at[at_cut], swap_recv.at[at_cut], me.mate,
+        ))
+        swaps[-1].start()
+    for cut in cuts:
+        multiply(near, core, False, cut)
+        multiply(far, core, False, cut)
 
     waiting = True
     pl.when(me.away)(own_send.wait_send)
@@ -243,18 +252,22 @@
             low_step(distance, sign)
     for load in load_tokens:
         load.wait()
-    swap.wait()
 
     index = me.pipe * Z + z
     target = labels[...] - index * rows
     peak = jnp.full((1, tokens), -jnp.inf, jnp.float32)
     picked = jnp.zeros((1, tokens), jnp.float32)
-    parts = spans(rows, 128)
+    parts = [
+        (cut + start, size) for cut, length in cuts for start, size in spans(length, 128)
+    ]
 
     def is_target(start, size):
         return lax.broadcasted_iota(jnp.int32, (size, tokens), 0) + start == target
 
     for start, size in parts:
+        for swap, cut in zip(swaps, cuts):
+            if start == cut[0]:
+                swap.wait_recv()
         where = pl.ds(start, size)
         logits = partial[core, where] + partial_in[where]
         partial_in[where] = logits
@@ -299,7 +312,7 @@
         share = jnp.exp(partial_in[where] - row_peak) * inverse
         hit = jnp.where(is_target(start, size), 1.0, 0.0)
         grads[core, where] = (scale * (share - hit)).astype(jnp.bfloat16)
-    share_grad = remote(grads.at[core], grads.at[core], mate_sems.at[2], mate_sems.at[3], me.mate)
+    share_grad = remote(grads.at[core], grads.at[core], mate_sems.at[0], mate_sems.at[1], me.mate)
     share_grad.start()
 
     def keep(half, sem):
@@ -331,6 +344,8 @@
     reduce_rows(me, block, term, hidden_out, lambda: lax.fori_loop(0, 4, back_rest, 0), *reduce_scratch)
 
     lax.fori_loop(1, n, wait_stat_send, 0)
+    for swap in swaps:
+        swap.wait_send()
     share_grad.wait_send()
     keep(core, out_sems.at[1]).wait()
     keep(1 - core, out_sems.at[2]).wait()
@@ -340,6 +355,8 @@
 def head(hidden_t, head_weight, labels, loss_weight, n):
     block, tokens = hidden_t.shape
     rows, width = head_weight.shape
+    padded = -(-rows // 8) * 8
+    low = block // 100 * 16
     dma = pltpu.SemaphoreType.DMA
 
     def pieces(count):
@@ -359,17 +376,18 @@
         scratch_shapes=[
             pltpu.VMEM((width, 2 * tokens), jnp.bfloat16),
             pltpu.VMEM((rows, width), jnp.bfloat16),
-            pltpu.VMEM((2, rows, tokens), jnp.float32),
-            pltpu.VMEM((rows, tokens), jnp.float32),
+            pltpu.VMEM((2, padded, tokens), jnp.float32),
+            pltpu.VMEM((padded, tokens), jnp.float32),
             pltpu.VMEM((2, rows, tokens), jnp.bfloat16),
             pltpu.VMEM((width, 2 * tokens), jnp.bfloat16),
             pltpu.VMEM((n, 8, tokens), jnp.float32),
             pltpu.VMEM((1, tokens), jnp.int32),
             pltpu.VMEM((1, tokens), jnp.float32),
             dma((16,)), dma((16,)), dma((8,)), dma((8,)), dma((16,)), dma((16,)), dma((8,)), dma((8,)), dma((4,)),
-            dma, dma, dma((4,)), dma((n,)), dma((n,)), dma((3,)), dma((2,)),
+            dma, dma, dma((2,)), dma((2,)), dma((2,)), dma((n,)), dma((n,)), dma((3,)), dma((2,)),
             pieces(12), pieces(8), pieces(8), pieces(8), pieces(4), pieces(8), one, one,
-            dma((12,)), dma((8,)), dma((8,)), dma((8,)), dma,
+            pltpu.VMEM((16, low, tokens), jnp.bfloat16), pieces(4),
+            dma((12,)), dma((8,)), dma((8,)), dma((8,)), dma, dma((16,)), dma((16,)),
             dma((4,)), dma((4,)), dma((12,)), dma((8,)), dma,
         ],
         compiler_params=pltpu.CompilerParams(
@@ -380,44 +398,85 @@
 
 def reduce_rows(
     me, block, term, out, finish_term,
-    from_y, from_x, from_below, from_above, passed, summed, final, landed,
-    recv_y, recv_x, recv_below, recv_above, recv_final,
+    from_y, from_x, from_below, from_above, passed, summed, final, landed, from_low, at_home,
+    recv_y, recv_x, recv_below, recv_above, recv_final, recv_low, send_low,
     send_x, send_pass, send_y, send_z, send_final,
 ):
     tokens = out.shape[1]
     x, z, core = me.x, me.z, me.core
 
-    def own(column, level, half):
-        start = pl.multiple_of((column * Z + level) * block, block)
-        return term.at[pl.ds(start, block), pl.ds(pl.multiple_of(half * tokens, tokens), tokens)]
-
-    upper = z // 2
-    order = (3 * (1 - upper), 2 - upper, 1 - z + 4 * upper, z)
-
-    def away_cross(level):
-        return remote(own(1 - x, level, 0), from_x.at[level * 2], send_x.at[level], recv_x.at[level * 2], me.x_peer)
-
-    def away_diagonal(level):
-        return remote(own(1 - x, level, 1), from_y.at[8 + level], send_y.at[8 + level], recv_y.at[8 + level], me.y_peer)
-
-    def away_line(level, half):
+    low = from_low.shape[1]
+    whole, upper, lower = (0, block), (low, block - low), (0, low)
+
+    top = z // 2
+    order = (3 * (1 - top), 2 - top, 1 - z + 4 * top, z)
+    last = Z - 1
+
+    def own(column, level, half, part):
+        start = pl.multiple_of((column * Z + level) * block + part[0], 16)
+        return term.at[pl.ds(start, part[1]), pl.ds(pl.multiple_of(half * tokens, tokens), tokens)]
+
+    def cut(ref, turn, slot):
+        start, size = whole if turn == last else upper
+        return ref.at[slot, pl.ds(start, size)]
+
+    def mine(peer, turn, half):
+        if turn == last:
+            return at_home.at[peer * 2 + half]
+        return own(1 - x if peer else x, order[turn], half, upper)
+
+    def away_cross(turn):
+        level = order[turn]
+        slot = level * 2
+        return remote(mine(1, turn, 0), cut(from_x, turn, slot), send_x.at[level], recv_x.at[slot], me.x_peer)
+
+    def away_diagonal(turn):
+        slot = 8 + order[turn]
+        return remote(mine(1, turn, 1), cut(from_y, turn, slot), send_y.at[slot], recv_y.at[slot], me.y_peer)
+
+    def away_line(turn, half):
+        slot = order[turn] * 2 + half
+        source = mine(0, turn, 1) if half else cut(passed, turn, order[turn])
+        return remote(source, cut(from_y, turn, slot), send_y.at[slot], recv_y.at[slot], me.y_peer)
+
+    def home_cross(turn, half):
+        level = order[turn]
         slot = level * 2 + half
-        source = own(x, level, 1) if half else passed.at[level]
-        return remote(source, from_y.at[slot], send_y.at[slot], recv_y.at[slot], me.y_peer)
-
-    def home_cross(level, half):
-        slot = level * 2 + half
-        source = passed.at[level] if half else own(1 - x, level, 0)
+        source = cut(passed, turn, level) if half else mine(1, turn, 0)
         sem = send_pass.at[level] if half else send_x.at[level]
-        return remote(source, from_x.at[slot], sem, recv_x.at[slot], me.x_peer)
+        return remote(source, cut(from_x, turn, slot), sem, recv_x.at[slot], me.x_peer)
 
     def rise(level, half):
         slot = level * 2 + half
-        return remote(summed.at[slot], from_below.at[slot], send_z.at[slot], recv_below.at[slot], me.up)
+        return remote(cut(summed, 0, slot), cut(from_below, 0, slot), send_z.at[slot], recv_below.at[slot], me.up)
 
     def sink(level, half):
         slot = level * 2 + half
-        return remote(summed.at[slot], from_above.at[slot], send_z.at[slot], recv_above.at[slot], me.down)
+        return remote(cut(summed, 0, slot), cut(from_above, 0, slot), send_z.at[slot], recv_above.at[slot], me.down)
+
+    def low_copy(turn, which):
+        level = order[turn]
+        source = own(x + which // 2 * (1 - 2 * x), level, which % 2, lower)
+        slot, there = z * 4 + which, level * 4 + which
+        return remote(source, from_low.at[slot], send_low.at[there], recv_low.at[slot], {"tensor": level})
+
+    def each_low(act):
+        def step(which, carry):
+            act(which)
+            return carry
+
+        lax.fori_loop(0, 4, step, 0)
+
+    def settle(which):
+        column, half = x + which // 2 * (1 - 2 * x), which % 2
+        total = f32(own(column, z, half, lower))
+        for step in range(1, Z):
+            slot = (z + step) % Z * 4 + which
+            here = from_low.at[slot]
+            remote(here, here, send_final, recv_low.at[slot], me.mate).wait_recv()
+            total += f32(here)
+        at_home[which, pl.ds(0, low)] = total.astype(jnp.bfloat16)
+        at_home[which, pl.ds(low, block - low)] = own(column, z, half, upper)[...]
 
     def hand_over():
         return remote(final, landed, send_final, recv_final, me.mate)
@@ -425,109 +484,141 @@
     def f32(ref):
         return ref[...].astype(jnp.float32)
 
+    for turn in (0, 1):
+        each_low(lambda which: low_copy(turn, which).start())
+
     @pl.when(me.away)
     def _():
-        for level in order[:2]:
-            away_cross(level).start()
-            away_diagonal(level).start()
-            away_line(level, 1).start()
+        for turn in (0, 1):
+            away_cross(turn).start()
+            away_diagonal(turn).start()
+            away_line(turn, 1).start()
 
     @pl.when(me.home)
     def _():
-        for level in order[:2]:
-            home_cross(level, 0).start()
+        for turn in (0, 1):
+            home_cross(turn, 0).start()
 
     finish_term()
+    each_low(lambda which: low_copy(2, which).start())
+
+    def away_turn(turn):
+        level = order[turn]
+        away_cross(turn).wait_recv()
+        cut(passed, turn, level)[...] = (
+            f32(mine(0, turn, 0)) + f32(cut(from_x, turn, level * 2))
+        ).astype(jnp.bfloat16)
+        away_line(turn, 0).start()
+        if turn + 2 < Z:
+            away_cross(turn + 2).start()
+            away_diagonal(turn + 2).start()
+            away_line(turn + 2, 1).start()
+
+    def pass_on(turn):
+        level = order[turn]
+        away_diagonal(turn).wait_recv()
+        cut(passed, turn, level)[...] = (
+            f32(mine(1, turn, 1)) + f32(cut(from_y, turn, 8 + level))
+        ).astype(jnp.bfloat16)
+        home_cross(turn, 1).start()
+
+    def gather(turn, half):
+        slot = order[turn] * 2 + half
+        total = f32(mine(0, turn, half))
+        for inbox, sems in ((from_y, recv_y), (from_x, recv_x)):
+            here = cut(inbox, turn, slot)
+            remote(here, here, send_final, sems.at[slot], me.mate).wait_recv()
+            total += f32(here)
+        return total
+
+    def send_on(turn):
+        level = order[turn]
+        for half in (1, 0):
+            slot = level * 2 + half
+            total = gather(turn, half)
+            kept = cut(summed, turn, slot)
+            kept[...] = total.astype(jnp.bfloat16)
+
+            @pl.when((level < z) & (z < Z - 1))
+            def _():
+                sink(level, half).wait_recv()
+                kept[...] = (total + f32(cut(from_above, turn, slot))).astype(jnp.bfloat16)
+
+            @pl.when((level > z) & (z > 0))
+            def _():
+                rise(level, half).wait_recv()
+                kept[...] = (total + f32(cut(from_below, turn, slot))).astype(jnp.bfloat16)
+
+            pl.when(level < z)(lambda: sink(level, half).start())
+            pl.when(level > z)(lambda: rise(level, half).start())
+
+    def finish(half, ref):
+        slot = z * 2 + half
+        total = gather(last, half)
+        ref[pl.ds(0, low)] = total[:low].astype(jnp.bfloat16)
+        rest, there = total[low:], pl.ds(low, block - low)
+        above, below = cut(from_above, 0, slot), cut(from_below, 0, slot)
+
+        @pl.when(z == 0)
+        def _():
+            sink(z, half).wait_recv()
+            ref[there] = (rest + f32(above)).astype(jnp.bfloat16)
+
+        @pl.when(z == Z - 1)
+        def _():
+            rise(z, half).wait_recv()
+            ref[there] = (rest + f32(below)).astype(jnp.bfloat16)
+
+        @pl.when((z > 0) & (z < Z - 1))
+        def _():
+            sink(z, half).wait_recv()
+            rise(z, half).wait_recv()
+            ref[there] = (rest + f32(above) + f32(below)).astype(jnp.bfloat16)
+
+    pl.when(me.away)(lambda: away_turn(0))
+
+    @pl.when(me.home)
+    def _():
+        pass_on(0)
+        home_cross(2, 0).start()
+        pass_on(1)
+
+    each_low(settle)
 
     @pl.when(me.away)
     def _():
-        for at, level in enumerate(order):
-            away_cross(level).wait_recv()
-            passed[level] = (f32(own(x, level, 0)) + f32(from_x.at[level * 2])).astype(jnp.bfloat16)
-            away_line(level, 0).start()
-            if at + 2 < Z:
-                away_cross(order[at + 2]).start()
-                away_diagonal(order[at + 2]).start()
-                away_line(order[at + 2], 1).start()
-        for level in order:
-            away_cross(level).wait_send()
-            away_diagonal(level).wait_send()
-            away_line(level, 1).wait_send()
-            away_line(level, 0).wait_send()
+        for turn in (1, 2, 3):
+            away_turn(turn)
+        for turn in range(Z):
+            away_cross(turn).wait_send()
+            away_diagonal(turn).wait_send()
+            away_line(turn, 1).wait_send()
+            away_line(turn, 0).wait_send()
         hand_over().wait_recv()
         out[...] = landed[...]
 
     @pl.when(me.home)
     def _():
-        def pass_on(level):
-            away_diagonal(level).wait_recv()
-            passed[level] = (f32(own(1 - x, level, 1)) + f32(from_y.at[8 + level])).astype(jnp.bfloat16)
-            home_cross(level, 1).start()
-
-        def gather(level, half):
-            slot = level * 2 + half
-            for inbox, sems in ((from_y, recv_y), (from_x, recv_x)):
-                remote(final, inbox.at[slot], send_final, sems.at[slot], me.mate).wait_recv()
-            return f32(own(x, level, half)) + f32(from_y.at[slot]) + f32(from_x.at[slot])
-
-        def send_on(level):
-            for half in (1, 0):
-                slot = level * 2 + half
-                total = gather(level, half)
-                summed[slot] = total.astype(jnp.bfloat16)
-
-                @pl.when((level < z) & (z < Z - 1))
-                def _():
-                    sink(level, half).wait_recv()
-                    summed[slot] = (total + f32(from_above.at[slot])).astype(jnp.bfloat16)
-
-                @pl.when((level > z) & (z > 0))
-                def _():
-                    rise(level, half).wait_recv()
-                    summed[slot] = (total + f32(from_below.at[slot])).astype(jnp.bfloat16)
-
-                pl.when(level < z)(lambda: sink(level, half).start())
-                pl.when(level > z)(lambda: rise(level, half).start())
-
-        pass_on(order[0])
-        home_cross(order[2], 0).start()
-        pass_on(order[1])
-        send_on(order[0])
-        home_cross(order[3], 0).start()
-        pass_on(order[2])
-        send_on(order[1])
-        pass_on(order[3])
-        send_on(order[2])
-
-        def finish(half, ref):
-            slot = z * 2 + half
-            total = gather(z, half)
-
-            @pl.when(z == 0)
-            def _():
-                sink(z, half).wait_recv()
-                ref[...] = (total + f32(from_above.at[slot])).astype(jnp.bfloat16)
-
-            @pl.when(z == Z - 1)
-            def _():
-                rise(z, half).wait_recv()
-                ref[...] = (total + f32(from_below.at[slot])).astype(jnp.bfloat16)
-
-            @pl.when((z > 0) & (z < Z - 1))
-            def _():
-                sink(z, half).wait_recv()
-                rise(z, half).wait_recv()
-                ref[...] = (total + f32(from_above.at[slot]) + f32(from_below.at[slot])).astype(jnp.bfloat16)
-
+        send_on(0)
+        home_cross(3, 0).start()
+        pass_on(2)
+        send_on(1)
+        pass_on(3)
+        send_on(2)
         finish(1 - core, final)
         hand_over().start()
         finish(core, out)
-        for level in order:
+        for turn in range(Z):
+            level = order[turn]
             for half in (0, 1):
-                home_cross(level, half).wait_send()
-                pl.when(level < z)(lambda: sink(level, half).wait_send())
-                pl.when(level > z)(lambda: rise(level, half).wait_send())
+                home_cross(turn, half).wait_send()
+                if turn < last:
+                    pl.when(level < z)(lambda: sink(level, half).wait_send())
+                    pl.when(level > z)(lambda: rise(level, half).wait_send())
         hand_over().wait_send()
+
+    for turn in range(last):
+        each_low(lambda which: low_copy(turn, which).wait_send())
 
 
 def per_device_chips(n, hidden, head_weight, labels, loss_weight):

time: 90 us -> 87.7 us (0.974)
  Pallas kernels: 80.5 us -> 78.1 us
    pallas_call x1, Pallas kernels: 80.5 us -> 78.1 us  [head(): pl.pallas_call(functools.partial(head_kernel, n, block), out_shape=(jax.S...]
where the time goes in v3:
time: 87.7 us; the launch traced here: 87.5 us
  Pallas kernels  78.1 us (89%)
  matrix products  5.24 us (6%)
  local copies, waits for them, and re-layouts  3.49 us (4%)
    pallas_call x1, Pallas kernels, head(): pl.pallas_call(functools.partial(head_kernel, n, block), out_shape=(jax.S...  78.1 us
    dot_general x1, matrix products, per_device_chips(): lax.dot_general(logit_grad, features, (((1,), (1,)), ((), ())), preferred...  5.24 us
    unnamed x8, local copies, waits for them, and re-layouts  3.49 us

profile of v3, /device:TPU:0, one launch (start us, length us, event | category | flops | bytes accessed | tf_op | source)
XLA Modules:
  0.0 87.5 jit_solution(4411235811100283898)
XLA Ops:
  0.6 0.0 copy-start
  0.6 0.9 %copy-done = bf16[256,320]{0,1:T(8,128)(2,1)S(1)} copy-done((bf16[256,320]{0,1:T(8,128)(2,1)S(1)}, bf16[256,320]{0,1:T(8,128)(2,1)}, u32[]{:S(2)}) %copy-start) | copy-done | bytes 163864
  1.5 0.0 copy-start.1
  1.6 0.7 copy-done.1
  2.2 0.0 copy-start.2
  2.2 0.7 copy-done.2
  2.9 78.1 %shard_map.67 = (bf16[2560,512]{1,0:T(8,128)(2,1)S(1)}, bf16[1187,512]{1,0:T(8,128)(2,1)S(1)}, f32[1,256]{1,0:T(1,128)S(1)}, bf16[320,256]{1,0:T(8,128)(2,1)S(1)}) custom-call(bf16[320,256]{1,0:T(8,128)(2,1)S(1)} %bitcast.7, bf16[1187,2560]{1,0:T(8,128)(2,1)} %weight.1, s32[1,256]{1,0:T(1,128)S(1)} %bitcast.9, f32[1,256]{1,0:T(1,128)S(1)} %bitcast.10), custom_call_target="tpu_custom_call" | custom-call | tf_op jit(solution)/shard_map/pallas_call | solution.py:366
  81.0 5.2 %convolution_convert_fusion = bf16[1187,2560]{1,0:T(8,128)(2,1)} fusion(bf16[1187,512]{1,0:T(8,128)(2,1)S(1)} %get-tuple-element.8, bf16[2560,512]{1,0:T(8,128)(2,1)S(1)} %get-tuple-element.9), kind=kOutput, calls=%fused_computation | convolution fusion | flops 3114688000 | bytes 9914368 | tf_op jit(solution)/shard_map/dot_general | solution.py:629
  86.3 0.7 copy.9
  86.9 0.6 copy.10
Async XLA Ops:
  0.6 0.9 %copy-start = (bf16[256,320]{0,1:T(8,128)(2,1)S(1)}, bf16[256,320]{0,1:T(8,128)(2,1)}, u32[]{:S(2)}) copy-start(bf16[256,320]{0,1:T(8,128)(2,1)} %param.4) | copy-start | bytes 491524
  1.5 0.7 copy-start.1
  2.2 0.7 copy-start.2

commit v4 on v3

--- a/solution.py
+++ b/solution.py
@@ -240,16 +240,6 @@
         multiply(near, core, False, cut)
         multiply(far, core, False, cut)
 
-    waiting = True
-    pl.when(me.away)(own_send.wait_send)
-    first_step()
-    peer_step(0, 1)
-    low_step(0, 0)
-    for distance in (1, 2, 3):
-        for sign in (-1, 1):
-            line_step(distance, sign)
-            peer_step(distance, sign)
-            low_step(distance, sign)
     for load in load_tokens:
         load.wait()
 
@@ -299,6 +289,17 @@
         return carry
 
     lax.fori_loop(1, n, send_stat, 0)
+    waiting = True
+    pl.when(me.away)(own_send.wait_send)
+    first_step()
+    peer_step(0, 1)
+    low_step(0, 0)
+    for distance in (1, 2, 3):
+        for sign in (-1, 1):
+            line_step(distance, sign)
+            peer_step(distance, sign)
+            low_step(distance, sign)
+
     lax.fori_loop(1, n, wait_stat, 0)
     every = stats[...]
     peaks, totals, picks = every[:, 0], every[:, 1], every[:, 2]

time: 87.7 us -> 87.4 us (level)
  no operation moved by 1% of the time
where the time goes in v4:
time: 87.4 us; the launch traced here: 87.2 us
  Pallas kernels  77.8 us (89%)
  matrix products  5.24 us (6%)
  local copies, waits for them, and re-layouts  3.49 us (4%)
    pallas_call x1, Pallas kernels, head(): pl.pallas_call(functools.partial(head_kernel, n, block), out_shape=(jax.S...  77.8 us
    dot_general x1, matrix products, per_device_chips(): lax.dot_general(logit_grad, features, (((1,), (1,)), ((), ())), preferred...  5.24 us
    unnamed x8, local copies, waits for them, and re-layouts  3.49 us

profile of v4, /device:TPU:0, one launch (start us, length us, event | category | flops | bytes accessed | tf_op | source)
XLA Modules:
  0.0 87.2 jit_solution(9856781898094368962)
XLA Ops:
  0.6 0.0 copy-start
  0.6 0.9 %copy-done = bf16[256,320]{0,1:T(8,128)(2,1)S(1)} copy-done((bf16[256,320]{0,1:T(8,128)(2,1)S(1)}, bf16[256,320]{0,1:T(8,128)(2,1)}, u32[]{:S(2)}) %copy-start) | copy-done | bytes 163864
  1.5 0.0 copy-start.1
  1.6 0.7 copy-done.1
  2.2 0.0 copy-start.2
  2.2 0.7 copy-done.2
  2.9 77.8 %shard_map.67 = (bf16[2560,512]{1,0:T(8,128)(2,1)S(1)}, bf16[1187,512]{1,0:T(8,128)(2,1)S(1)}, f32[1,256]{1,0:T(1,128)S(1)}, bf16[320,256]{1,0:T(8,128)(2,1)S(1)}) custom-call(bf16[320,256]{1,0:T(8,128)(2,1)S(1)} %bitcast.7, bf16[1187,2560]{1,0:T(8,128)(2,1)} %weight.1, s32[1,256]{1,0:T(1,128)S(1)} %bitcast.9, f32[1,256]{1,0:T(1,128)S(1)} %bitcast.10), custom_call_target="tpu_custom_call" | custom-call | tf_op jit(solution)/shard_map/pallas_call | solution.py:367
  80.7 5.2 %convolution_convert_fusion = bf16[1187,2560]{1,0:T(8,128)(2,1)} fusion(bf16[1187,512]{1,0:T(8,128)(2,1)S(1)} %get-tuple-element.8, bf16[2560,512]{1,0:T(8,128)(2,1)S(1)} %get-tuple-element.9), kind=kOutput, calls=%fused_computation | convolution fusion | flops 3114688000 | bytes 9914368 | tf_op jit(solution)/shard_map/dot_general | solution.py:630
  86.0 0.7 copy.9
  86.7 0.6 copy.10
Async XLA Ops:
  0.6 0.9 %copy-start = (bf16[256,320]{0,1:T(8,128)(2,1)S(1)}, bf16[256,320]{0,1:T(8,128)(2,1)}, u32[]{:S(2)}) copy-start(bf16[256,320]{0,1:T(8,128)(2,1)} %param.4) | copy-start | bytes 491524
  1.5 0.7 copy-start.1
  2.2 0.7 copy-start.2
